TPU v7x, 32 devices: a whole 2x2x4 slice. The times are simulated.
32 devices in a mesh: grp: 2 (over y), row: 4 (over z), view: 2 (over x), col: 2 (over core).
Axes of the slice: x: 2, y: 2, z: 4, core: 2. Of those that a mesh axis runs over, the one named last changes fastest.
Arguments:
- omega: bfloat16 [16384, 256], P('row', 'col'), may hold values from -6 to 6
- neighbor_ids: int32 [2, 10, 32768], P('view', None, ('grp', 'row')), parts along dimension 2, may hold values from 0 to 1151
- degrees: int32 [2, 32768], P('view', ('grp', 'row')), parts along dimension 1, may hold values from 10 to 39
Outputs:
- basis: float32 [32768, 256], P(('grp', 'row', 'view'), 'col'), parts along dimension 0
- factor: float32 [512, 256], P('grp', 'col'), parts along dimension 0
There are 2 independent parts, one for each index of `grp`. A program takes and returns all parts, laid end to end along the dimension named above; an argument that names none is the same for every part. Nothing has to cross between parts.
All inputs are finite; a program needn't handle non-finite values.
Results may differ from a plain program's by a relative error of at most 0.0052.
Values may be sent and summed in bfloat16 or wider, within the bound.
A program may use at most 64 MiB of HBM per device.

v0:
```python
import math

import jax
import jax.numpy as jnp
from jax import lax
from jax.sharding import PartitionSpec as P

TILE = 128
BAND = 4


def with_halo(array, sides, width):
    for axis, dim in sides:
        count, length = (lax.axis_size(axis), array.shape[dim])
        up = [(i, (i + 1) % count) for i in range(count - 1)]
        down = [(j, i) for i, j in up]
        last = lax.slice_in_dim(array, length - width, length, axis=dim)
        first = lax.slice_in_dim(array, 0, width, axis=dim)
        before = lax.ppermute(last, axis, up)
        after = lax.ppermute(first, axis, down)
        array = jnp.concatenate([before, array, after], axis=dim)
    return array


def band_product(padded, window_ids, row_count):
    tile_count = row_count // TILE
    tiled_ids = window_ids.reshape(window_ids.shape[0], tile_count, TILE)
    positions = jnp.arange(TILE, dtype=jnp.int32)
    result = jnp.zeros((tile_count, TILE, padded.shape[1]), jnp.float32)
    for offset in range(2 * BAND + 1):
        counts = jnp.zeros((tile_count, TILE, TILE), jnp.bfloat16)
        for slot_index in range(tiled_ids.shape[0]):
            counts = counts + (
                tiled_ids[slot_index][:, :, None] == offset * TILE + positions
            ).astype(jnp.bfloat16)
        shifted = padded[offset * TILE : offset * TILE + row_count].reshape(tile_count, TILE, -1)
        result = result + jnp.einsum(
            "tij,tjc->tic", counts, shifted, preferred_element_type=jnp.float32
        )
    return result.reshape(row_count, -1)


def propagate(sketch, window_ids, inv_root):
    row_count = sketch.shape[0]
    scaled = (inv_root[:, None] * sketch.astype(jnp.float32)).astype(jnp.bfloat16)
    padded = with_halo(scaled, (("row", 0),), BAND * TILE)
    return inv_root[:, None] * band_product(padded, window_ids, row_count)


def total_gram(all_columns):
    partial_gram = jnp.einsum(
        "rk,rj->kj", all_columns, all_columns, precision=lax.Precision.HIGHEST
    )
    summed_gram = lax.psum(partial_gram, "row")
    return summed_gram


def shards(omega, neighbor_ids, degrees):
    inv_root = 1.0 / jnp.sqrt(degrees[0].astype(jnp.float32))
    window_ids = neighbor_ids[0]
    sketch = omega
    summed = None
    for sweep in range(2):
        view_terms = propagate(sketch, window_ids, inv_root)
        summed = lax.psum(view_terms, "view")
        if sweep == 0:
            rounded = summed.astype(jnp.bfloat16)
            sketch = rounded
    all_columns = lax.all_gather(summed, "col", axis=1, tiled=True)
    gram_matrix = total_gram(all_columns)
    lower_factor = jnp.linalg.cholesky(gram_matrix)
    quarter_count = summed.shape[0] // lax.axis_size("view")
    own_rows = lax.dynamic_slice_in_dim(
        all_columns, lax.axis_index("view") * quarter_count, quarter_count, 0
    )
    solved = jax.scipy.linalg.solve_triangular(lower_factor, own_rows.T, lower=True)
    width_share = summed.shape[1]
    start_column = lax.axis_index("col") * width_share
    row_scale = math.sqrt(omega.shape[0] * lax.axis_size("row"))
    basis = lax.dynamic_slice_in_dim(solved, start_column, width_share, 0).T * row_scale
    factor = lax.dynamic_slice_in_dim(lower_factor.T, start_column, width_share, 1) / row_scale
    return (basis, factor)


def solution(mesh):
    return jax.shard_map(
        shards,
        mesh=mesh,
        in_specs=(P("row", "col"), P("view", None, ("grp", "row")), P("view", ("grp", "row"))),
        out_specs=(P(("grp", "row", "view"), "col"), P("grp", "col")),
        check_vma=False,
    )
```

profile of v0, /device:TPU:0, one launch (start us, length us, event | category | flops | bytes accessed | tf_op | source)
XLA Modules:
  0.0 445.9 jit_solution(11939392170635712311)
XLA Ops:
  7.2 0.8 convert_rsqrt_fusion
  8.0 1.7 multiply_convert_fusion.1
  9.8 4.9 %collective-permute-start = (bf16[512,128]{1,0:T(8,128)(2,1)S(1)}, bf16[512,128]{1,0:T(8,128)(2,1)S(1)}, u32[]{:S(2)}, u32[]{:S(2)}) collective-permute-start(bf16[512,128]{1,0:T(8,128)(2,1)S(1)} %get-tuple-element.50), channel_id=1, source_target_pairs={{0,4},{4,8},{8,12},{1,5},{5,9},{9,13},{2,6},{6,10},{10,14},{3,7},{... | collective-permute-start | bytes 393224 | tf_op jit(solution)/shard_map/ppermute | solution.py:19
  14.7 1.3 collective-permute-start.1
  16.1 5.8 %fusion.135 = f32[32,128,128]{2,1,0:T(8,128)S(1)} fusion(bf16[32,128,128]{2,1,0:T(8,128)(2,1)S(1)} %bitcast.90, s32[128]{0:T(128)S(1)} %iota_add_fusion.4, s32[32,128]{1,0:T(8,128)S(1)} %bitcast.256, s32[32,128]{1,0:T(8,128)S(1)} %bitcast.274, s32[32,128]{1,0:T(8,128)S(1)} %bitcast.130, s32[32,128]{1,0:T(8,128)S(1)} %bitcast.148, ...), kind=kOutput, calls=%fused_computation.258 | convolution fusion | flops 149422080 | bytes 3310080 | tf_op jit(solution)/shard_map/tij,tjc->tic/dot_general | solution.py:37
  22.0 18.4 %pad_maximum_fusion.2 = (bf16[4096,128]{1,0:T(8,128)(2,1)S(1)}, bf16[4096,128]{1,0:T(8,128)(2,1)S(1)}, bf16[4096,128]{1,0:T(8,128)(2,1)S(1)}, bf16[4096,128]{1,0...) fusion(bf16[512,128]{1,0:T(8,128)(2,1)S(1)} %collective-permute, ...), kind=kLoop, calls=%fused_computation.225 | loop fusion | flops 16777216 | bytes 9699328 | tf_op jit(solution)/shard_map/concatenate | solution.py:21
  40.4 18.0 %fusion.112 = f32[32,128,128]{2,1,0:T(8,128)S(1)} fusion(bf16[32,128,128]{2,1,0:T(8,128)(2,1)S(1)} %bitcast.107, s32[32,128]{1,0:T(8,128)S(1)} %bitcast.257, s32[32,128]{1,0:T(8,128)S(1)} %bitcast.275, s32[32,128]{1,0:T(8,128)S(1)} %bitcast.131, s32[32,128]{1,0:T(8,128)S(1)} %bitcast.149, s32[32,128]{1,0:T(8,128)S(1)} %bitcast.167, ...), kind=kOutput, calls=%fused_computation.234 | convolution fusion | flops 155189248 | bytes 3309568 | tf_op jit(solution)/shard_map/tij,tjc->tic/dot_general | solution.py:37
  58.4 5.8 %fusion.127 = f32[32,128,128]{2,1,0:T(8,128)S(1)} fusion(bf16[32,128,128]{2,1,0:T(8,128)(2,1)S(1)} %bitcast.105, s32[128]{0:T(128)S(1)} %iota_add_fusion.2, s32[32,128]{1,0:T(8,128)S(1)} %bitcast.258, s32[32,128]{1,0:T(8,128)S(1)} %bitcast.276, s32[32,128]{1,0:T(8,128)S(1)} %bitcast.132, s32[32,128]{1,0:T(8,128)S(1)} %bitcast.150, ...), kind=kOutput, calls=%fused_computation.254 | convolution fusion | flops 149422080 | bytes 3310080 | tf_op jit(solution)/shard_map/tij,tjc->tic/dot_general | solution.py:37
  64.2 6.0 %fusion.131 = f32[32,128,128]{2,1,0:T(8,128)S(1)} fusion(bf16[32,128,128]{2,1,0:T(8,128)(2,1)S(1)} %bitcast.104, s32[128]{0:T(128)S(1)} %iota_add_fusion.3, s32[32,128]{1,0:T(8,128)S(1)} %bitcast.259, s32[32,128]{1,0:T(8,128)S(1)} %bitcast.277, s32[32,128]{1,0:T(8,128)S(1)} %bitcast.133, s32[32,128]{1,0:T(8,128)S(1)} %bitcast.151, ...), kind=kOutput, calls=%fused_computation.256 | convolution fusion | flops 149422080 | bytes 3310080 | tf_op jit(solution)/shard_map/tij,tjc->tic/dot_general | solution.py:37
  70.2 5.8 %fusion.139 = f32[32,128,128]{2,1,0:T(8,128)S(1)} fusion(bf16[32,128,128]{2,1,0:T(8,128)(2,1)S(1)} %bitcast.102, s32[128]{0:T(128)S(1)} %iota_add_fusion.5, s32[32,128]{1,0:T(8,128)S(1)} %bitcast.260, s32[32,128]{1,0:T(8,128)S(1)} %bitcast.278, s32[32,128]{1,0:T(8,128)S(1)} %bitcast.134, s32[32,128]{1,0:T(8,128)S(1)} %bitcast.152, ...), kind=kOutput, calls=%fused_computation.260 | convolution fusion | flops 149422080 | bytes 3310080 | tf_op jit(solution)/shard_map/tij,tjc->tic/dot_general | solution.py:37
  76.0 5.8 %fusion.143 = f32[32,128,128]{2,1,0:T(8,128)S(1)} fusion(bf16[32,128,128]{2,1,0:T(8,128)(2,1)S(1)} %bitcast.101, s32[128]{0:T(128)S(1)} %iota_add_fusion.6, s32[32,128]{1,0:T(8,128)S(1)} %bitcast.261, s32[32,128]{1,0:T(8,128)S(1)} %bitcast.279, s32[32,128]{1,0:T(8,128)S(1)} %bitcast.135, s32[32,128]{1,0:T(8,128)S(1)} %bitcast.153, ...), kind=kOutput, calls=%fused_computation.262 | convolution fusion | flops 149422080 | bytes 3310080 | tf_op jit(solution)/shard_map/tij,tjc->tic/dot_general | solution.py:37
  81.9 5.8 %fusion.147 = f32[32,128,128]{2,1,0:T(8,128)S(1)} fusion(bf16[32,128,128]{2,1,0:T(8,128)(2,1)S(1)} %bitcast.99, s32[128]{0:T(128)S(1)} %iota_add_fusion.7, s32[32,128]{1,0:T(8,128)S(1)} %bitcast.262, s32[32,128]{1,0:T(8,128)S(1)} %bitcast.280, s32[32,128]{1,0:T(8,128)S(1)} %bitcast.136, s32[32,128]{1,0:T(8,128)S(1)} %bitcast.154, ...), kind=kOutput, calls=%fused_computation.264 | convolution fusion | flops 149422080 | bytes 3310080 | tf_op jit(solution)/shard_map/tij,tjc->tic/dot_general | solution.py:37
  87.7 6.2 %fusion.123 = f32[32,128,128]{2,1,0:T(8,128)S(1)} fusion(bf16[32,128,128]{2,1,0:T(8,128)(2,1)S(1)} %bitcast.98, s32[128]{0:T(128)S(1)} %iota_add_fusion.1, s32[32,128]{1,0:T(8,128)S(1)} %bitcast.263, s32[32,128]{1,0:T(8,128)S(1)} %bitcast.281, s32[32,128]{1,0:T(8,128)S(1)} %bitcast.137, s32[32,128]{1,0:T(8,128)S(1)} %bitcast.155, ...), kind=kOutput, calls=%fused_computation.252 | convolution fusion | flops 149422080 | bytes 3310080 | tf_op jit(solution)/shard_map/tij,tjc->tic/dot_general | solution.py:37
  93.9 5.8 %add_add_fusion.1 = f32[32,128,128]{2,1,0:T(8,128)S(1)} fusion(f32[32,128,128]{2,1,0:T(8,128)S(1)} %fusion.123, f32[32,128,128]{2,1,0:T(8,128)S(1)} %fusion.127, f32[32,128,128]{2,1,0:T(8,128)S(1)} %fusion.131, f32[32,128,128]{2,1,0:T(8,128)S(1)} %fusion.135, f32[32,128,128]{2,1,0:T(8,128)S(1)} %fusion.139, f32[32,128,128]{2,1,0:T(8,128)S(1)} %fusion.143, ...), kind=kOutput, calls=%fused_computation.10 | convolution fusion | flops 153616384 | bytes 20087296 | tf_op jit(solution)/shard_map/tij,tjc->tic/dot_general | solution.py:37
  100.4 52.1 %all-reduce.8 = bf16[4096,128]{1,0:T(8,128)(2,1)S(1)} all-reduce(f32[4096,128]{1,0:T(8,128)S(1)} %bitcast_multiply_fusion.1), channel_id=1, replica_groups=mesh['grp'=2,'row'=4,'view'=2,'col'=2] {'view'}, use_global_device_ids=true, to_apply=%region_0.0 | all-reduce | flops 524288 | bytes 3145728 | tf_op jit(solution)/shard_map/psum | solution.py:65
  152.5 0.7 multiply_convert_fusion
  153.3 4.0 collective-permute-start.2
  157.2 1.3 collective-permute-start.3
  158.5 6.0 %fusion.133 = f32[32,128,128]{2,1,0:T(8,128)S(1)} fusion(bf16[32,128,128]{2,1,0:T(8,128)(2,1)S(1)} %bitcast.91, s32[128]{0:T(128)S(1)} %iota_add_fusion.4, s32[32,128]{1,0:T(8,128)S(1)} %bitcast.265, s32[32,128]{1,0:T(8,128)S(1)} %bitcast.283, s32[32,128]{1,0:T(8,128)S(1)} %bitcast.139, s32[32,128]{1,0:T(8,128)S(1)} %bitcast.157, ...), kind=kOutput, calls=%fused_computation.257 | convolution fusion | flops 149422080 | bytes 3310080 | tf_op jit(solution)/shard_map/tij,tjc->tic/dot_general | solution.py:37
  164.6 18.4 %pad_maximum_fusion = (bf16[4096,128]{1,0:T(8,128)(2,1)S(1)}, bf16[4096,128]{1,0:T(8,128)(2,1)S(1)}, bf16[4096,128]{1,0:T(8,128)(2,1)S(1)}, bf16[4096,128]{1,0:T...) fusion(bf16[512,128]{1,0:T(8,128)(2,1)S(1)} %collective-permute, ...), kind=kLoop, calls=%fused_computation.223 | loop fusion | flops 16777216 | bytes 9699328 | tf_op jit(solution)/shard_map/concatenate | solution.py:21
  183.0 5.8 %fusion.125 = f32[32,128,128]{2,1,0:T(8,128)S(1)} fusion(bf16[32,128,128]{2,1,0:T(8,128)(2,1)S(1)} %bitcast.106, s32[128]{0:T(128)S(1)} %iota_add_fusion.2, s32[32,128]{1,0:T(8,128)S(1)} %bitcast.266, s32[32,128]{1,0:T(8,128)S(1)} %bitcast.284, s32[32,128]{1,0:T(8,128)S(1)} %bitcast.140, s32[32,128]{1,0:T(8,128)S(1)} %bitcast.158, ...), kind=kOutput, calls=%fused_computation.253 | convolution fusion | flops 149422080 | bytes 3310080 | tf_op jit(solution)/shard_map/tij,tjc->tic/dot_general | solution.py:37
  188.8 6.2 %fusion.129 = f32[32,128,128]{2,1,0:T(8,128)S(1)} fusion(bf16[32,128,128]{2,1,0:T(8,128)(2,1)S(1)} %bitcast.103, s32[128]{0:T(128)S(1)} %iota_add_fusion.3, s32[32,128]{1,0:T(8,128)S(1)} %bitcast.267, s32[32,128]{1,0:T(8,128)S(1)} %bitcast.285, s32[32,128]{1,0:T(8,128)S(1)} %bitcast.141, s32[32,128]{1,0:T(8,128)S(1)} %bitcast.159, ...), kind=kOutput, calls=%fused_computation.255 | convolution fusion | flops 149422080 | bytes 3310080 | tf_op jit(solution)/shard_map/tij,tjc->tic/dot_general | solution.py:37
  195.0 5.8 %fusion.137 = f32[32,128,128]{2,1,0:T(8,128)S(1)} fusion(bf16[32,128,128]{2,1,0:T(8,128)(2,1)S(1)} %bitcast.100, s32[128]{0:T(128)S(1)} %iota_add_fusion.5, s32[32,128]{1,0:T(8,128)S(1)} %bitcast.268, s32[32,128]{1,0:T(8,128)S(1)} %bitcast.286, s32[32,128]{1,0:T(8,128)S(1)} %bitcast.142, s32[32,128]{1,0:T(8,128)S(1)} %bitcast.160, ...), kind=kOutput, calls=%fused_computation.259 | convolution fusion | flops 149422080 | bytes 3310080 | tf_op jit(solution)/shard_map/tij,tjc->tic/dot_general | solution.py:37
  200.9 5.8 %fusion.141 = f32[32,128,128]{2,1,0:T(8,128)S(1)} fusion(bf16[32,128,128]{2,1,0:T(8,128)(2,1)S(1)} %bitcast.97, s32[128]{0:T(128)S(1)} %iota_add_fusion.6, s32[32,128]{1,0:T(8,128)S(1)} %bitcast.269, s32[32,128]{1,0:T(8,128)S(1)} %bitcast.287, s32[32,128]{1,0:T(8,128)S(1)} %bitcast.143, s32[32,128]{1,0:T(8,128)S(1)} %bitcast.161, ...), kind=kOutput, calls=%fused_computation.261 | convolution fusion | flops 149422080 | bytes 3310080 | tf_op jit(solution)/shard_map/tij,tjc->tic/dot_general | solution.py:37
  206.7 5.8 %fusion.145 = f32[32,128,128]{2,1,0:T(8,128)S(1)} fusion(bf16[32,128,128]{2,1,0:T(8,128)(2,1)S(1)} %bitcast.96, s32[128]{0:T(128)S(1)} %iota_add_fusion.7, s32[32,128]{1,0:T(8,128)S(1)} %bitcast.270, s32[32,128]{1,0:T(8,128)S(1)} %bitcast.288, s32[32,128]{1,0:T(8,128)S(1)} %bitcast.144, s32[32,128]{1,0:T(8,128)S(1)} %bitcast.162, ...), kind=kOutput, calls=%fused_computation.263 | convolution fusion | flops 149422080 | bytes 3310080 | tf_op jit(solution)/shard_map/tij,tjc->tic/dot_general | solution.py:37
  212.5 17.9 %fusion.110 = f32[32,128,128]{2,1,0:T(8,128)S(1)} fusion(bf16[32,128,128]{2,1,0:T(8,128)(2,1)S(1)} %bitcast.95, s32[32,128]{1,0:T(8,128)S(1)} %bitcast.271, s32[32,128]{1,0:T(8,128)S(1)} %bitcast.289, s32[32,128]{1,0:T(8,128)S(1)} %bitcast.145, s32[32,128]{1,0:T(8,128)S(1)} %bitcast.163, s32[32,128]{1,0:T(8,128)S(1)} %bitcast.181, ...), kind=kOutput, calls=%fused_computation.233 | convolution fusion | flops 155189248 | bytes 3309568 | tf_op jit(solution)/shard_map/tij,tjc->tic/dot_general | solution.py:37
  230.5 6.0 %fusion.121 = f32[32,128,128]{2,1,0:T(8,128)S(1)} fusion(bf16[32,128,128]{2,1,0:T(8,128)(2,1)S(1)} %bitcast.94, s32[128]{0:T(128)S(1)} %iota_add_fusion.1, s32[32,128]{1,0:T(8,128)S(1)} %bitcast.272, s32[32,128]{1,0:T(8,128)S(1)} %bitcast.290, s32[32,128]{1,0:T(8,128)S(1)} %bitcast.146, s32[32,128]{1,0:T(8,128)S(1)} %bitcast.164, ...), kind=kOutput, calls=%fused_computation.251 | convolution fusion | flops 149422080 | bytes 3310080 | tf_op jit(solution)/shard_map/tij,tjc->tic/dot_general | solution.py:37
  236.5 5.8 %add_add_fusion = f32[32,128,128]{2,1,0:T(8,128)S(1)} fusion(f32[32,128,128]{2,1,0:T(8,128)S(1)} %fusion.121, f32[32,128,128]{2,1,0:T(8,128)S(1)} %fusion.125, f32[32,128,128]{2,1,0:T(8,128)S(1)} %fusion.129, f32[32,128,128]{2,1,0:T(8,128)S(1)} %fusion.133, f32[32,128,128]{2,1,0:T(8,128)S(1)} %fusion.137, f32[32,128,128]{2,1,0:T(8,128)S(1)} %fusion.141, ...), kind=kOutput, calls=%fused_computation.8 | convolution fusion | flops 153616384 | bytes 20087296 | tf_op jit(solution)/shard_map/tij,tjc->tic/dot_general | solution.py:37
  242.3 1.9 bitcast_multiply_fusion
  244.3 64.6 %all-reduce.5.cloned.1.call-done = f32[4096,128]{1,0:T(8,128)} async-done(((f32[4096,128]{1,0:T(8,128)}), f32[4096,128]{1,0:T(8,128)}) %all-reduce.5.cloned.1.call-update) | async-done | bytes 2097168 | tf_op jit(solution)/shard_map/psum | solution.py:65
  309.0 14.5 %all-gather.2.cloned.1.call-done = f32[4096,256]{1,0:T(8,128)} async-done(((f32[4096,128]{1,0:T(8,128)}), f32[4096,256]{1,0:T(8,128)}) %all-gather.2.cloned.1.call-update) | async-done | bytes 4194320 | tf_op jit(solution)/shard_map/all_gather | solution.py:69
  323.5 10.9 %fusion.153 = f32[256,256]{0,1:T(8,128)} fusion(f32[4096,256]{1,0:T(8,128)} %all-gather.2.cloned.1.call-done), kind=kOutput, calls=%fused_computation.279 | convolution fusion | flops 3221225472 | bytes 4456448 | tf_op jit(solution)/shard_map/rk,rj->kj/dot_general | solution.py:51
  334.5 1.7 dynamic-slice_bitcast_fusion
  336.2 35.0 %all-reduce.7.cloned.1.call-done = f32[256,256]{0,1:T(8,128)} async-done(((f32[256,256]{0,1:T(8,128)}), f32[256,256]{0,1:T(8,128)}) %all-reduce.7.cloned.1.call-update) | async-done | bytes 262160 | tf_op jit(solution)/shard_map/psum | solution.py:54
  371.2 1.1 copy.6
  372.2 1.0 fusion.108
  373.2 11.7 %cholesky.50 = f32[128,128]{1,0:T(8,128)S(1)} custom-call(f32[128,128]{1,0:T(8,128)S(1)} %cholesky.118), custom_call_target="Cholesky" | custom-call | tf_op jit(solution)/shard_map/jit(cholesky)/cholesky | solution.py:71
  385.0 10.0 %custom-call.15 = f32[1,128,128]{1,2,0:T(8,128)S(1)} custom-call(f32[1,128,128]{2,1,0:T(8,128)S(1)} %get-tuple-element.65), custom_call_target="InvertDiagBlocksLowerTriangular" | custom-call | tf_op jit(solution)/shard_map/jit(cholesky)/cholesky | solution.py:71
  395.5 11.7 %cholesky.105 = f32[128,128]{1,0:T(8,128)S(1)} custom-call(f32[128,128]{1,0:T(8,128)S(1)} %convolution_subtract_fusion.1), custom_call_target="Cholesky" | custom-call | tf_op jit(solution)/shard_map/jit(cholesky)/cholesky | solution.py:71
  409.2 3.8 while.1
  409.8 1.3 bitcast_dynamic-update-slice_fusion.2
  411.7 1.3 bitcast_dynamic-update-slice_fusion.2
  413.0 19.7 %custom-call.16 = f32[2,128,128]{1,2,0:T(8,128)S(1)} custom-call(f32[2,128,128]{2,1,0:T(8,128)S(1)} %get-tuple-element.9), custom_call_target="InvertDiagBlocksLowerTriangular" | custom-call | tf_op jit(solution)/shard_map/jit(_solve_triangular)/triangular_solve | solution.py:76
  432.7 1.1 fusion.106
  433.8 1.8 convolution_subtract_fusion
  435.6 1.1 fusion.115
  436.9 1.3 copy.7
  438.3 0.8 copy.8
  (41 shorter events, 3.6 us)
Async XLA Ops:
  7.2 8.9 %copy-start = (s32[1,10,4096]{2,0,1:T(1,128)S(1)}, s32[1,10,4096]{2,0,1:T(1,128)}, u32[]{:S(2)}) copy-start(s32[1,10,4096]{2,0,1:T(1,128)} %param.4) | copy-start | bytes 491524
  7.2 301.8 %all-reduce.5.cloned.1.call-start = ((), (), s32[]{:S(2)}) async-start(), calls=%async_computation | async-start | bytes 4194304 | tf_op jit(solution)/shard_map/psum | solution.py:65
  9.8 12.2 %collective-permute-start = (bf16[512,128]{1,0:T(8,128)(2,1)S(1)}, bf16[512,128]{1,0:T(8,128)(2,1)S(1)}, u32[]{:S(2)}, u32[]{:S(2)}) collective-permute-start(bf16[512,128]{1,0:T(8,128)(2,1)S(1)} %get-tuple-element.50), channel_id=1, source_target_pairs={{0,4},{4,8},{8,12},{1,5},{5,9},{9,13},{2,6},{6,10},{10,14},{3,7},{... | collective-permute-start | bytes 393224 | tf_op jit(solution)/shard_map/ppermute | solution.py:19
  14.7 7.3 %collective-permute-start.1 = (bf16[512,128]{1,0:T(8,128)(2,1)S(1)}, bf16[512,128]{1,0:T(8,128)(2,1)S(1)}, u32[]{:S(2)}, u32[]{:S(2)}) collective-permute-start(bf16[512,128]{1,0:T(8,128)(2,1)S(1)} %get-tuple-element.51), channel_id=1, source_target_pairs={{4,0},{8,4},{12,8},{5,1},{9,5},{13,9},{6,2},{10,6},{14,10},{7,3},{... | collective-permute-start | bytes 393224 | tf_op jit(solution)/shard_map/ppermute | solution.py:20
  153.3 11.3 %collective-permute-start.2 = (bf16[512,128]{1,0:T(8,128)(2,1)S(1)}, bf16[512,128]{1,0:T(8,128)(2,1)S(1)}, u32[]{:S(2)}, u32[]{:S(2)}) collective-permute-start(bf16[512,128]{1,0:T(8,128)(2,1)S(1)} %get-tuple-element.44), channel_id=1, source_target_pairs={{0,4},{4,8},{8,12},{1,5},{5,9},{9,13},{2,6},{6,10},{10,14},{3,7},{... | collective-permute-start | bytes 393224 | tf_op jit(solution)/shard_map/ppermute | solution.py:19
  157.2 7.3 %collective-permute-start.3 = (bf16[512,128]{1,0:T(8,128)(2,1)S(1)}, bf16[512,128]{1,0:T(8,128)(2,1)S(1)}, u32[]{:S(2)}, u32[]{:S(2)}) collective-permute-start(bf16[512,128]{1,0:T(8,128)(2,1)S(1)} %get-tuple-element.45), channel_id=1, source_target_pairs={{4,0},{8,4},{12,8},{5,1},{9,5},{13,9},{6,2},{10,6},{14,10},{7,3},{... | collective-permute-start | bytes 393224 | tf_op jit(solution)/shard_map/ppermute | solution.py:20
  244.3 79.3 %all-gather.2.cloned.1.call-start = ((), (), s32[]{:S(2)}) async-start(), calls=%async_computation.1 | async-start | bytes 6291456 | tf_op jit(solution)/shard_map/all_gather | solution.py:69
  308.9 62.2 %all-reduce.7.cloned.1.call-start = ((), (), s32[]{:S(2)}) async-start(), calls=%async_computation.2 | async-start | bytes 524288 | tf_op jit(solution)/shard_map/psum | solution.py:54
Sparse Core Ops, SparseCore 0:
  244.4 64.4 all-reduce.4
  310.5 12.9 all-gather.1
  334.6 36.5 all-reduce.6
where the time goes:
time: 455 us; the launch traced here: 446 us
  matrix products  146 us (32%)
  waiting for transfers between devices  114 us (25%)
  other arithmetic  97.7 us (21%)
  blocking collectives  52.1 us (11%)
  between operations  15.7 us (3%)
  starting transfers between devices  11.6 us (3%)
  local copies, waits for them, and re-layouts  8.81 us (2%)
    dot_general x18, matrix products, band_product(): jnp.einsum('tij,tjc->tic', counts, shifted, preferred_element_type=jnp.fl...  131 us
    psum x1, waiting for transfers between devices, shards(): summed = lax.psum(view_terms, 'view')  64.6 us
    psum x1, blocking collectives, shards(): summed = lax.psum(view_terms, 'view')  52.1 us
    concatenate x2, other arithmetic, with_halo(): array = jnp.concatenate([before, array, after], axis=dim)  36.8 us
    psum x1, waiting for transfers between devices, total_gram(): summed_gram = lax.psum(partial_gram, 'row')  35 us
    another operation x6, other arithmetic, shards(): lower_factor = jnp.linalg.cholesky(gram_matrix)  34.1 us
    another operation x3, other arithmetic, shards(): jax.scipy.linalg.solve_triangular(lower_factor, own_rows.T, lower=True)  19.7 us
    all_gather x1, waiting for transfers between devices, shards(): all_columns = lax.all_gather(summed, 'col', axis=1, tiled=True)  14.5 us
  transfers between devices with their start and end apart: 7, of which 3 were waited for; matrix products, arithmetic and copies ran while one was open for 3% of the time, Pallas kernels for 0%

commit v1 on v0

v1 whole, which is shorter than its diff:
```python
import functools
import math

import jax
import jax.numpy as jnp
from jax import lax
from jax.experimental import pallas as pl
from jax.experimental.pallas import tpu as pltpu
from jax.sharding import PartitionSpec as P

TILE = 128
BAND = 4
HALO = TILE * BAND
PAIR = 2 * TILE
SPAN = PAIR + 2 * HALO
FIELDS = SPAN // TILE
BLOCK = 32
MESH = pl.DeviceIdType.MESH
HIGHEST = lax.Precision.HIGHEST


def sketch_kernel(
    zs, vs, omega_ref, ids_ref, deg_ref, both_ref, gram_ref,
    om, ids, deg, inv, counts, scaled, first,
    local_sems, ids_sems, deg_sems, om_sems, edge_sems, edge_deg_sems, halo_sems, both_sems,
):
    grp, r, v, c = (lax.axis_index(a) for a in ("grp", "row", "view", "col"))
    total = zs * vs * 2
    length = omega_ref.shape[0]
    own = length // (2 * vs)
    wide = own + 2 * HALO
    slots = ids_ref.shape[1]
    half = omega_ref.shape[1]
    place = (r * vs + v) * 2 + c
    base = pl.multiple_of((v * 2 + c) * own, HALO)

    def at(index):
        return (grp, index // (2 * vs), (index // 2) % vs, index % 2)

    def remote(src, dst, sems, slot_index, device):
        return pltpu.make_async_remote_copy(
            src_ref=src, dst_ref=dst, send_sem=sems.at[0, slot_index], recv_sem=sems.at[1, slot_index],
            device_id=device, device_id_type=MESH,
        )

    own_ids = pltpu.make_async_copy(ids_ref.at[0, :, pl.ds(base, own)], ids.at[0], local_sems.at[0])
    own_deg = pltpu.make_async_copy(deg_ref, deg.at[0, :, pl.ds(HALO, length)], local_sems.at[1])
    own_om = pltpu.make_async_copy(omega_ref, om.at[c, pl.ds(HALO, length), :], local_sems.at[2])
    own_ids.start()
    own_deg.start()
    own_om.start()

    barrier = pltpu.get_barrier_semaphore()

    def greet(i, carry):
        pl.semaphore_signal(barrier, inc=1, device_id=at((place + i) % total), device_id_type=MESH)
        return carry

    lax.fori_loop(1, total, greet, 0)
    pl.semaphore_wait(barrier, total - 1)

    sends = []
    for k in range(1, vs):
        w = (v + vs - k) % vs
        there = (grp, r, w, c)
        piece = pl.multiple_of((w * 2 + c) * own, HALO)
        sends.append(remote(ids_ref.at[0, :, pl.ds(piece, own)], ids.at[k], ids_sems, k - 1, there))
        sends.append(remote(deg_ref, deg.at[k, :, pl.ds(HALO, length)], deg_sems, k - 1, there))
    window = min(wide, length)
    other_base = (v * 2 + 1 - c) * own
    start = pl.multiple_of(jnp.clip(other_base - HALO, 0, length - window), HALO)
    om_copy = remote(
        omega_ref.at[pl.ds(start, window), :], om.at[c, pl.ds(HALO + start, window), :],
        om_sems, 0, (grp, r, v, 1 - c),
    )
    my_start = pl.multiple_of(jnp.clip(base - HALO, 0, length - window), HALO)
    om_arrive = remote(
        omega_ref.at[pl.ds(start, window), :], om.at[1 - c, pl.ds(HALO + my_start, window), :],
        om_sems, 0, (grp, r, v, 1 - c),
    )
    up_ok = r < zs - 1
    down_ok = r > 0
    next_row = jnp.minimum(r + 1, zs - 1)
    prev_row = jnp.maximum(r - 1, 0)
    low, high = pl.ds(0, HALO), pl.ds(HALO + length, HALO)
    last = pl.ds(length - HALO, HALO)
    firsts = pl.ds(0, HALO)
    edge_up = remote(omega_ref.at[last, :], om.at[c, low, :], edge_sems, c, (grp, next_row, 0, 0))
    edge_down = remote(omega_ref.at[firsts, :], om.at[c, high, :], edge_sems, c, (grp, prev_row, vs - 1, 1))
    slot_up = v
    slot_down = (v + 1) % vs
    deg_up = remote(deg_ref.at[:, last], deg.at[slot_up, :, low], edge_deg_sems, slot_up, (grp, next_row, 0, 0))
    deg_down = remote(
        deg_ref.at[:, firsts], deg.at[slot_down, :, high], edge_deg_sems, slot_down, (grp, prev_row, vs - 1, 1)
    )
    send_edge_up = up_ok & (v == 0)
    send_edge_down = down_ok & (v == vs - 1)
    send_deg_up = up_ok & (c == 0)
    send_deg_down = down_ok & (c == 1)
    get_low = down_ok & (v == 0) & (c == 0)
    get_high = up_ok & (v == vs - 1) & (c == 1)

    pl.when(send_edge_up)(edge_up.start)
    pl.when(send_edge_down)(edge_down.start)
    for s in sends:
        s.start()
    pl.when(send_deg_up)(deg_up.start)
    pl.when(send_deg_down)(deg_down.start)
    om_copy.start()

    @pl.when(r == 0)
    def _():
        om[:, low, :] = jnp.zeros((2, HALO, half), om.dtype)
        deg[:, :, low] = jnp.ones((vs, 1, HALO), deg.dtype)

    @pl.when(r == zs - 1)
    def _():
        om[:, high, :] = jnp.zeros((2, HALO, half), om.dtype)
        deg[:, :, high] = jnp.ones((vs, 1, HALO), deg.dtype)

    def build(k):
        def one(d, carry):
            mine = ids[k, :, pl.ds(pl.multiple_of(d * PAIR, PAIR), PAIR)]
            lane = lax.broadcasted_iota(jnp.int32, mine.shape, 1)
            tile = (mine >> 7) + jnp.where(lane >= TILE, 1, 0)
            within = mine & (TILE - 1)
            one_a = jnp.where(tile < 8, jnp.int32(1) << (4 * jnp.minimum(tile, 7)), 0)
            one_b = jnp.where(tile >= 8, jnp.int32(1) << (4 * jnp.maximum(tile - 8, 0)), 0)
            rows = 32
            for p in range(TILE // rows):
                spot = lax.broadcasted_iota(jnp.int32, (rows, PAIR), 0) + p * rows
                acc_a = jnp.zeros((rows, PAIR), jnp.int32)
                acc_b = jnp.zeros((rows, PAIR), jnp.int32)
                for s in range(slots):
                    hit = within[s : s + 1, :] == spot
                    acc_a = acc_a + jnp.where(hit, one_a[s : s + 1, :], 0)
                    acc_b = acc_b + jnp.where(hit, one_b[s : s + 1, :], 0)
                for h in range(FIELDS):
                    acc = acc_a if h < 8 else acc_b
                    field = (acc >> (4 * (h % 8))) & 15
                    counts[k, d, h * TILE + p * rows : h * TILE + (p + 1) * rows, :] = field.astype(
                        jnp.float32
                    ).astype(jnp.bfloat16)
            return carry

        lax.fori_loop(0, own // PAIR, one, 0)

    own_ids.wait()
    build(0)
    for k in range(1, vs):
        sends[2 * (k - 1)].wait_recv()
        build(k)
    for k in range(1, vs):
        sends[2 * (k - 1) + 1].wait_recv()
    own_deg.wait()
    own_om.wait()
    om_arrive.wait_recv()

    @pl.when(get_low)
    def _():
        for h in range(2):
            remote(omega_ref.at[last, :], om.at[h, low, :], edge_sems, h, (grp, prev_row, 0, 0)).wait_recv()
        for k in range(vs):
            remote(deg_ref.at[:, last], deg.at[k, :, low], edge_deg_sems, k, (grp, prev_row, 0, 0)).wait_recv()

    @pl.when(get_high)
    def _():
        for h in range(2):
            remote(omega_ref.at[firsts, :], om.at[h, high, :], edge_sems, h, (grp, next_row, 0, 0)).wait_recv()
        for k in range(vs):
            remote(deg_ref.at[:, firsts], deg.at[k, :, high], edge_deg_sems, k, (grp, next_row, 0, 0)).wait_recv()

    for k in range(vs):
        inv[k] = 1.0 / jnp.sqrt(deg[k, :, pl.ds(base, wide)].astype(jnp.float32))

    def turn(i, carry):
        lanes = pl.ds(pl.multiple_of(i * PAIR, PAIR), PAIR)
        for h in range(2):
            part = om[h, pl.ds(pl.multiple_of(base + i * PAIR, PAIR), PAIR), :].astype(jnp.float32).T
            for k in range(vs):
                scaled[k, h * half : (h + 1) * half, lanes] = (inv[k, :, lanes] * part).astype(jnp.bfloat16)
        return carry

    lax.fori_loop(0, wide // PAIR, turn, 0)

    def product(d):
        out = None
        for k in range(vs):
            term = jnp.dot(
                scaled[k, :, pl.ds(pl.multiple_of(d * PAIR, PAIR), SPAN)], counts[k, d],
                preferred_element_type=jnp.float32,
            )
            term = inv[k, :, pl.ds(pl.multiple_of(HALO + d * PAIR, PAIR), PAIR)] * term
            out = term if out is None else out + term
        return out

    def sweep_one(d, carry):
        first[:, pl.ds(pl.multiple_of(HALO + d * PAIR, PAIR), PAIR)] = product(d).astype(jnp.bfloat16)
        return carry

    before = at(jnp.maximum(place - 1, 0))
    after = at(jnp.minimum(place + 1, total - 1))
    down = remote(first.at[:, pl.ds(HALO, HALO)], first.at[:, pl.ds(HALO + own, HALO)], halo_sems, 0, before)
    up = remote(first.at[:, pl.ds(own, HALO)], first.at[:, pl.ds(0, HALO)], halo_sems, 1, after)
    has_before, has_after = place > 0, place < total - 1

    lax.fori_loop(0, HALO // PAIR, sweep_one, 0)
    pl.when(has_before)(down.start)
    lax.fori_loop(HALO // PAIR, own // PAIR, sweep_one, 0)
    pl.when(has_after)(up.start)

    @pl.when(place == 0)
    def _():
        first[:, pl.ds(0, HALO)] = jnp.zeros((2 * half, HALO), first.dtype)

    @pl.when(place == total - 1)
    def _():
        first[:, pl.ds(HALO + own, HALO)] = jnp.zeros((2 * half, HALO), first.dtype)

    def rescale(i, carry):
        lanes = pl.ds(pl.multiple_of(i * PAIR, PAIR), PAIR)
        part = first[:, lanes].astype(jnp.float32)
        for k in range(vs):
            scaled[k, :, lanes] = (inv[k, :, lanes] * part).astype(jnp.bfloat16)
        return carry

    lax.fori_loop(HALO // PAIR, (HALO + own) // PAIR, rescale, 0)
    pl.when(has_before)(up.wait_recv)
    lax.fori_loop(0, HALO // PAIR, rescale, 0)
    pl.when(has_after)(down.wait_recv)
    lax.fori_loop((HALO + own) // PAIR, wide // PAIR, rescale, 0)

    def sweep_two(d, carry):
        both_ref[:, pl.ds(pl.multiple_of(c * own + d * PAIR, PAIR), PAIR)] = product(d)
        return carry

    lax.fori_loop(0, own // PAIR, sweep_two, 0)
    mine = pl.ds(pl.multiple_of(c * own, PAIR), own)
    theirs = pl.ds(pl.multiple_of((1 - c) * own, PAIR), own)
    swap = remote(both_ref.at[:, mine], both_ref.at[:, mine], both_sems, 0, (grp, r, v, 1 - c))
    swap_in = remote(both_ref.at[:, mine], both_ref.at[:, theirs], both_sems, 0, (grp, r, v, 1 - c))
    swap.start()
    second = both_ref[:, mine]
    gram_ref[...] = lax.dot_general(
        second, second, (((1,), (1,)), ((), ())), precision=HIGHEST, preferred_element_type=jnp.float32
    )

    swap.wait_send()
    swap_in.wait_recv()
    for s in sends:
        s.wait_send()
    om_copy.wait_send()
    pl.when(send_edge_up)(edge_up.wait_send)
    pl.when(send_edge_down)(edge_down.wait_send)
    pl.when(send_deg_up)(deg_up.wait_send)
    pl.when(send_deg_down)(deg_down.wait_send)
    pl.when(has_before)(down.wait_send)
    pl.when(has_after)(up.wait_send)


def factor_kernel(scale, gram_ref, both_ref, basis_ref, factor_ref, work, upper, inverse):
    size = gram_ref.shape[0]
    c = lax.axis_index("col")
    half = size // 2
    work[:, :size] = gram_ref[...]
    work[:, size:] = jnp.where(
        lax.broadcasted_iota(jnp.int32, (size, size), 0) == lax.broadcasted_iota(jnp.int32, (size, size), 1),
        jnp.float32(1), jnp.float32(0),
    )
    rows = lax.broadcasted_iota(jnp.int32, (BLOCK, BLOCK), 0)
    cols = lax.broadcasted_iota(jnp.int32, (BLOCK, BLOCK), 1)
    for k in range(size // BLOCK):
        lo, hi = k * BLOCK, (k + 1) * BLOCK
        block = work[lo:hi, lo:hi]
        left = jnp.where(rows == cols, jnp.float32(1), jnp.float32(0))
        for j in range(BLOCK - 1):
            ratio = jnp.where(rows[:, :1] > j, block[:, j : j + 1] / block[j : j + 1, j : j + 1], 0.0)
            block, left = (block - ratio * block[j : j + 1, :], left - ratio * left[j : j + 1, :])
        pivots = jnp.sum(jnp.where(rows == cols, block, 0.0), axis=1, keepdims=True)
        left = left / jnp.sqrt(pivots)
        panel = jnp.dot(left, work[lo:hi, :], precision=HIGHEST, preferred_element_type=jnp.float32)
        row_index = lax.broadcasted_iota(jnp.int32, (BLOCK, size), 0) + lo
        col_index = lax.broadcasted_iota(jnp.int32, (BLOCK, size), 1)
        top = jnp.where(col_index >= row_index, panel[:, :size], 0.0)
        upper[lo:hi, :] = top
        inverse[lo:hi, :] = panel[:, size:]
        if hi < size:
            keep = hi // TILE * TILE
            update = lax.dot_general(
                top[:, keep:], panel, (((0,), (0,)), ((), ())),
                precision=HIGHEST, preferred_element_type=jnp.float32,
            )
            work[hi:, :] = work[hi:, :] - update[hi - keep :, :]
    factor_ref[...] = upper[:, pl.ds(pl.multiple_of(c * half, TILE), half)] * (1.0 / scale)
    share = inverse[pl.ds(pl.multiple_of(c * half, TILE), half), :] * scale

    def one(i, carry):
        spot = pl.multiple_of(i * PAIR, PAIR)
        part = jnp.dot(
            share, both_ref[:, pl.ds(spot, PAIR)], precision=HIGHEST, preferred_element_type=jnp.float32
        )
        basis_ref[pl.ds(spot, PAIR), :] = part.T
        return carry

    lax.fori_loop(0, both_ref.shape[1] // PAIR, one, 0)


def shards(omega, neighbor_ids, degrees):
    zs, vs = lax.axis_size("row"), lax.axis_size("view")
    length, half = omega.shape
    slots = neighbor_ids.shape[1]
    own = length // (2 * vs)
    wide = own + 2 * HALO
    size = 2 * half
    vmem = pl.BlockSpec(memory_space=pltpu.VMEM)
    anywhere = pl.BlockSpec(memory_space=pl.ANY)
    dma = pltpu.SemaphoreType.DMA
    both, gram = pl.pallas_call(
        functools.partial(sketch_kernel, zs, vs),
        out_shape=(
            jax.ShapeDtypeStruct((size, 2 * own), jnp.float32),
            jax.ShapeDtypeStruct((size, size), jnp.float32),
        ),
        in_specs=[anywhere] * 3,
        out_specs=(vmem, vmem),
        scratch_shapes=[
            pltpu.VMEM((2, length + 2 * HALO, half), jnp.bfloat16),
            pltpu.VMEM((vs, slots, own), jnp.int32),
            pltpu.VMEM((vs, 1, length + 2 * HALO), jnp.int32),
            pltpu.VMEM((vs, 1, wide), jnp.float32),
            pltpu.VMEM((vs, own // PAIR, SPAN, PAIR), jnp.bfloat16),
            pltpu.VMEM((vs, size, wide), jnp.bfloat16),
            pltpu.VMEM((size, wide), jnp.bfloat16),
            dma((3,)),
            dma((2, max(vs - 1, 1))),
            dma((2, max(vs - 1, 1))),
            dma((2, 1)),
            dma((2, 2)),
            dma((2, vs)),
            dma((2, 2)),
            dma((2, 1)),
        ],
        compiler_params=pltpu.CompilerParams(
            collective_id=0, has_side_effects=True, vmem_limit_bytes=40 * 1024 * 1024
        ),
        name="sketch",
    )(omega, neighbor_ids, degrees)
    gram = lax.psum(gram, ("row", "view", "col"))
    return pl.pallas_call(
        functools.partial(factor_kernel, math.sqrt(length * zs)),
        out_shape=(
            jax.ShapeDtypeStruct((2 * own, half), jnp.float32),
            jax.ShapeDtypeStruct((size, half), jnp.float32),
        ),
        in_specs=[vmem, vmem],
        out_specs=(vmem, vmem),
        scratch_shapes=[
            pltpu.VMEM((size, 2 * size), jnp.float32),
            pltpu.VMEM((size, size), jnp.float32),
            pltpu.VMEM((size, size), jnp.float32),
        ],
        compiler_params=pltpu.CompilerParams(vmem_limit_bytes=32 * 1024 * 1024),
        name="factor",
    )(gram, both)


def solution(mesh):
    return jax.shard_map(
        shards,
        mesh=mesh,
        in_specs=(P("row", "col"), P("view", None, ("grp", "row")), P("view", ("grp", "row"))),
        out_specs=(P(("grp", "row", "view"), "col"), P("grp", "col")),
        check_vma=False,
    )
```

time: 455 us -> 162 us (0.36); the launches traced: 446 us -> 162 us
  matrix products: 146 us -> 0 us
  other arithmetic: 97.7 us -> 0 us
  Pallas kernels: 0 us -> 53.9 us
  blocking collectives: 52.1 us -> 0 us
  waiting for transfers between devices: 114 us -> 89.7 us
  starting transfers between devices: 11.6 us -> 0.04 us
  local copies, waits for them, and re-layouts: 8.81 us -> 3.9 us
    dot_general x19 -> x0, matrix products: 141 us -> none  [the longest x18 131 us: band_product(): jnp.einsum('tij,tjc->tic', counts, shifted, preferred_element_type=jnp.fl...]
    pallas_call x0 -> x2, Pallas kernels: none -> 53.9 us  [the longest x1 30 us: shards(): pl.pallas_call(functools.partial(factor_kernel, math.sqrt(length * zs)),...]
    another operation x9 -> x0, other arithmetic: 53.8 us -> none  [the longest x6 34.1 us: shards(): lower_factor = jnp.linalg.cholesky(gram_matrix)]
    psum x1 -> x0, blocking collectives: 52.1 us -> none  [shards(): summed = lax.psum(view_terms, 'view')]
    concatenate x2 -> x0, other arithmetic: 36.8 us -> none  [with_halo(): array = jnp.concatenate([before, array, after], axis=dim)]
    all_gather x1 -> x0, waiting for transfers between devices: 14.5 us -> none  [shards(): all_columns = lax.all_gather(summed, 'col', axis=1, tiled=True)]
    ppermute x4 -> x0, starting transfers between devices: 11.5 us -> none  [the longest x2 8.91 us: with_halo(): before = lax.ppermute(last, axis, up)]
    psum x2 -> x1, waiting for transfers between devices: 99.5 us -> 89.7 us  [shards(): gram = lax.psum(gram, ('row', 'view', 'col'))]
  transfers between devices with their start and end apart: 7 -> 1, of which waited for: 3 -> 1; matrix products, arithmetic and copies ran while one was open for 3% -> 0% of each run, Pallas kernels for 0% -> 0%
where the time goes in v1:
time: 162 us
  waiting for transfers between devices  89.7 us (55%)
  Pallas kernels  53.9 us (33%)
  between operations  14 us (9%)
  local copies, waits for them, and re-layouts  3.9 us (2%)
    psum x1, waiting for transfers between devices, shards(): gram = lax.psum(gram, ('row', 'view', 'col'))  89.7 us
    pallas_call x1, Pallas kernels, shards(): pl.pallas_call(functools.partial(factor_kernel, math.sqrt(length * zs)),...  30 us
    pallas_call x1, Pallas kernels, shards(): pl.pallas_call(functools.partial(sketch_kernel, zs, vs), out_shape=(jax.S...  23.9 us
    unnamed x7, local copies, waits for them, and re-layouts  3.9 us
  transfers between devices with their start and end apart: 1, of which 1 were waited for; matrix products, arithmetic and copies ran while one was open for 0% of the time, Pallas kernels for 0%

profile of v1, /device:TPU:0, one launch (start us, length us, event | category | flops | bytes accessed | tf_op | source)
XLA Modules:
  0.0 161.6 jit_solution(3325406425036169782)
XLA Ops:
  7.2 0.0 all-reduce.2.cloned.1.call-start
  7.2 1.0 copy.5.ids_ref
  8.2 0.0 copy-start
  8.2 1.2 copy-done
  9.5 0.0 copy-start.2
  9.5 0.7 copy-done.2
  10.2 23.9 %sketch.1 = (f32[256,2048]{1,0:T(8,128)S(1)}, f32[256,256]{1,0:T(8,128)}) custom-call(bf16[4096,128]{1,0:T(8,128)(2,1)S(1)} %copy-done, s32[1,10,4096]{2,1,0:T(8,128)S(1)} %copy.5.ids_ref, s32[1,4096]{1,0:T(1,128)S(1)} %copy-done.2), custom_call_target="tpu_custom_call" | custom-call | tf_op jit(solution)/shard_map/sketch/pallas_call | solution.py:318
  34.1 0.0 all-reduce.2.cloned.1.call-update
  34.1 89.7 %all-reduce.2.cloned.1.call-done.gram_ref = f32[256,256]{1,0:T(8,128)} async-done(((f32[256,256]{1,0:T(8,128)}), f32[256,256]{1,0:T(8,128)}) %all-reduce.2.cloned.1.call-update) | async-done | bytes 262160 | tf_op jit(solution)/shard_map/psum | solution.py:348
  123.8 0.0 copy-start.1
  123.8 0.9 copy-done.1
  124.8 30.0 %factor.1 = (f32[2048,128]{1,0:T(8,128)}, f32[256,128]{1,0:T(8,128)}) custom-call(f32[256,256]{1,0:T(8,128)S(1)} %copy-done.1, f32[256,2048]{1,0:T(8,128)S(1)} %get-tuple-element.5.both_ref), custom_call_target="tpu_custom_call" | custom-call | tf_op jit(solution)/shard_map/factor/pallas_call | solution.py:349
Async XLA Ops:
  7.2 116.7 %all-reduce.2.cloned.1.call-start = ((), (), s32[]{:S(2)}) async-start(), calls=%async_computation | async-start | bytes 524288 | tf_op jit(solution)/shard_map/psum | solution.py:348
  8.2 1.2 copy-start
  9.5 0.7 copy-start.2
  123.8 0.9 copy-start.1
Sparse Core Ops, SparseCore 0:
  34.2 89.5 all-reduce.1

commit v2 on v1

--- a/solution.py
+++ b/solution.py
@@ -19,10 +19,15 @@
 HIGHEST = lax.Precision.HIGHEST
 
 
+def summed_inside(zs, vs):
+    return 3 * TILE % (2 * zs * vs * 8) == 0
+
+
 def sketch_kernel(
     zs, vs, omega_ref, ids_ref, deg_ref, both_ref, gram_ref,
-    om, ids, deg, inv, counts, scaled, first,
+    om, ids, deg, inv, counts, scaled, first, partial, arrived, pieces,
     local_sems, ids_sems, deg_sems, om_sems, edge_sems, edge_deg_sems, halo_sems, both_sems,
+    half_sems, piece_sems, spread_sems, join_sems,
 ):
     grp, r, v, c = (lax.axis_index(a) for a in ("grp", "row", "view", "col"))
     total = zs * vs * 2
@@ -240,14 +245,67 @@
     swap = remote(both_ref.at[:, mine], both_ref.at[:, mine], both_sems, 0, (grp, r, v, 1 - c))
     swap_in = remote(both_ref.at[:, mine], both_ref.at[:, theirs], both_sems, 0, (grp, r, v, 1 - c))
     swap.start()
-    second = both_ref[:, mine]
-    gram_ref[...] = lax.dot_general(
-        second, second, (((1,), (1,)), ((), ())), precision=HIGHEST, preferred_element_type=jnp.float32
-    )
+
+    target = partial if summed_inside(zs, vs) else gram_ref
+    inner = (((1,), (1,)), ((), ()))
+    left, right = both_ref[:half, mine], both_ref[half:, mine]
+    for i, (x, y) in enumerate(((left, left), (left, right), (right, right))):
+        target[i * half : (i + 1) * half, :] = lax.dot_general(
+            x, y, inner, precision=HIGHEST, preferred_element_type=jnp.float32
+        )
+    late = []
+    if summed_inside(zs, vs):
+        peers = zs * vs
+        share = 3 * half // 2
+        piece = share // peers
+        spot = r * vs + v
+        other = (grp, r, v, 1 - c)
+        own_share = pl.multiple_of(c * share, 8)
+        other_share = pl.multiple_of((1 - c) * share, 8)
+        cross = remote(partial.at[pl.ds(other_share, share), :], arrived, half_sems, 0, other)
+        cross.start()
+        cross.wait_recv()
+        late.append(cross)
+        partial[pl.ds(own_share, share), :] = partial[pl.ds(own_share, share), :] + arrived[...]
+
+        def link(src, dst, sems, sent_by, to):
+            return pltpu.make_async_remote_copy(
+                src_ref=src, dst_ref=dst, send_sem=sems.at[0, to], recv_sem=sems.at[1, sent_by],
+                device_id=(grp, to // vs, to % vs, c), device_id_type=MESH,
+            )
+
+        for i in range(1, peers):
+            to = (spot + i) % peers
+            rows = pl.ds(pl.multiple_of(own_share + to * piece, 8), piece)
+            copy = link(partial.at[rows, :], pieces.at[spot], piece_sems, spot, to)
+            copy.start()
+            late.append(copy)
+        own_rows = pl.ds(pl.multiple_of(own_share + spot * piece, 8), piece)
+        pieces[spot] = partial[own_rows, :]
+        for i in range(1, peers):
+            source = (spot + i) % peers
+            link(partial.at[own_rows, :], pieces.at[source], piece_sems, source, source).wait_recv()
+        whole = pieces[0]
+        for i in range(1, peers):
+            whole = whole + pieces[i]
+        gram_ref[own_rows, :] = whole
+        for i in range(1, peers):
+            copy = link(gram_ref.at[own_rows, :], gram_ref.at[own_rows, :], spread_sems, spot, (spot + i) % peers)
+            copy.start()
+            late.append(copy)
+        for i in range(1, peers):
+            source = (spot + i) % peers
+            rows = pl.ds(pl.multiple_of(own_share + source * piece, 8), piece)
+            link(gram_ref.at[own_rows, :], gram_ref.at[rows, :], spread_sems, source, source).wait_recv()
+        rows = pl.ds(own_share, share)
+        join = remote(gram_ref.at[rows, :], gram_ref.at[rows, :], join_sems, 0, other)
+        join.start()
+        remote(gram_ref.at[rows, :], gram_ref.at[pl.ds(other_share, share), :], join_sems, 0, other).wait_recv()
+        late.append(join)
 
     swap.wait_send()
     swap_in.wait_recv()
-    for s in sends:
+    for s in sends + late:
         s.wait_send()
     om_copy.wait_send()
     pl.when(send_edge_up)(edge_up.wait_send)
@@ -259,10 +317,13 @@
 
 
 def factor_kernel(scale, gram_ref, both_ref, basis_ref, factor_ref, work, upper, inverse):
-    size = gram_ref.shape[0]
+    size = 2 * gram_ref.shape[1]
     c = lax.axis_index("col")
     half = size // 2
-    work[:, :size] = gram_ref[...]
+    work[:half, :half] = gram_ref[:half, :]
+    work[:half, half:size] = gram_ref[half : 2 * half, :]
+    work[half:, :half] = jnp.zeros((half, half), jnp.float32)
+    work[half:, half:size] = gram_ref[2 * half :, :]
     work[:, size:] = jnp.where(
         lax.broadcasted_iota(jnp.int32, (size, size), 0) == lax.broadcasted_iota(jnp.int32, (size, size), 1),
         jnp.float32(1), jnp.float32(0),
@@ -312,6 +373,7 @@
     own = length // (2 * vs)
     wide = own + 2 * HALO
     size = 2 * half
+    peers = zs * vs
     vmem = pl.BlockSpec(memory_space=pltpu.VMEM)
     anywhere = pl.BlockSpec(memory_space=pl.ANY)
     dma = pltpu.SemaphoreType.DMA
@@ -319,7 +381,7 @@
         functools.partial(sketch_kernel, zs, vs),
         out_shape=(
             jax.ShapeDtypeStruct((size, 2 * own), jnp.float32),
-            jax.ShapeDtypeStruct((size, size), jnp.float32),
+            jax.ShapeDtypeStruct((3 * half, half), jnp.float32),
         ),
         in_specs=[anywhere] * 3,
         out_specs=(vmem, vmem),
@@ -331,6 +393,9 @@
             pltpu.VMEM((vs, own // PAIR, SPAN, PAIR), jnp.bfloat16),
             pltpu.VMEM((vs, size, wide), jnp.bfloat16),
             pltpu.VMEM((size, wide), jnp.bfloat16),
+            pltpu.VMEM((3 * half, half), jnp.float32),
+            pltpu.VMEM((3 * half // 2, half), jnp.float32),
+            pltpu.VMEM((peers, max(3 * half // 2 // peers, 1), half), jnp.float32),
             dma((3,)),
             dma((2, max(vs - 1, 1))),
             dma((2, max(vs - 1, 1))),
@@ -339,13 +404,18 @@
             dma((2, vs)),
             dma((2, 2)),
             dma((2, 1)),
+            dma((2, 1)),
+            dma((2, peers)),
+            dma((2, peers)),
+            dma((2, 1)),
         ],
         compiler_params=pltpu.CompilerParams(
             collective_id=0, has_side_effects=True, vmem_limit_bytes=40 * 1024 * 1024
         ),
         name="sketch",
     )(omega, neighbor_ids, degrees)
-    gram = lax.psum(gram, ("row", "view", "col"))
+    if not summed_inside(zs, vs):
+        gram = lax.psum(gram, ("row", "view", "col"))
     return pl.pallas_call(
         functools.partial(factor_kernel, math.sqrt(length * zs)),
         out_shape=(

time: 162 us -> 69 us (0.43)
  waiting for transfers between devices: 89.7 us -> 0 us
  between operations: 14 us -> 0.65 us
  Pallas kernels: 53.9 us -> 65.2 us
    psum x1 -> x0, waiting for transfers between devices: 89.7 us -> none  [shards(): gram = lax.psum(gram, ('row', 'view', 'col'))]
    pallas_call x1, Pallas kernels: 23.9 us -> 35.2 us  [shards(): pl.pallas_call(functools.partial(sketch_kernel, zs, vs), out_shape=(jax.S...]
    unnamed x7 -> x5, local copies, waits for them, and re-layouts: 3.9 us -> 2.95 us
  transfers between devices with their start and end apart: 1 -> 0, of which waited for: 1 -> 0; matrix products, arithmetic and copies ran while one was open for 0% -> 0% of each run, Pallas kernels for 0% -> 0%
where the time goes in v2:
time: 69 us; the launch traced here: 68.8 us
  Pallas kernels  65.2 us (94%)
  local copies, waits for them, and re-layouts  2.95 us (4%)
    pallas_call x1, Pallas kernels, shards(): pl.pallas_call(functools.partial(sketch_kernel, zs, vs), out_shape=(jax.S...  35.2 us
    pallas_call x1, Pallas kernels, shards(): pl.pallas_call(functools.partial(factor_kernel, math.sqrt(length * zs)),...  30 us
    unnamed x5, local copies, waits for them, and re-layouts  2.95 us

profile of v2, /device:TPU:0, one launch (start us, length us, event | category | flops | bytes accessed | tf_op | source)
XLA Modules:
  0.0 68.8 jit_solution(12703610783282927635)
XLA Ops:
  0.6 1.0 %copy.5.ids_ref = s32[1,10,4096]{2,1,0:T(8,128)S(1)} copy(s32[1,10,4096]{2,0,1:T(1,128)} %param.4) | data formatting | bytes 327680 | tf_op args[1]
  1.6 0.0 copy-start
  1.7 1.2 %copy-done = bf16[4096,128]{1,0:T(8,128)(2,1)S(1)} copy-done((bf16[4096,128]{1,0:T(8,128)(2,1)S(1)}, bf16[4096,128]{1,0:T(8,128)(2,1)}, u32[]{:S(2)}) %copy-start) | copy-done | bytes 1048600
  2.9 0.0 copy-start.1
  2.9 0.7 %copy-done.1 = s32[1,4096]{1,0:T(1,128)S(1)} copy-done((s32[1,4096]{1,0:T(1,128)S(1)}, s32[1,4096]{1,0:T(1,128)}, u32[]{:S(2)}) %copy-start.1) | copy-done | bytes 16408
  3.6 35.2 %sketch.1 = (f32[256,2048]{1,0:T(8,128)S(1)}, f32[384,128]{1,0:T(8,128)S(1)}) custom-call(bf16[4096,128]{1,0:T(8,128)(2,1)S(1)} %copy-done, s32[1,10,4096]{2,1,0:T(8,128)S(1)} %copy.5.ids_ref, s32[1,4096]{1,0:T(1,128)S(1)} %copy-done.1), custom_call_target="tpu_custom_call" | custom-call | tf_op jit(solution)/shard_map/sketch/pallas_call | solution.py:380
  38.8 30.0 %factor.1 = (f32[2048,128]{1,0:T(8,128)}, f32[256,128]{1,0:T(8,128)}) custom-call(f32[384,128]{1,0:T(8,128)S(1)} %get-tuple-element.4.gram_ref, f32[256,2048]{1,0:T(8,128)S(1)} %get-tuple-element.5.both_ref), custom_call_target="tpu_custom_call" | custom-call | tf_op jit(solution)/shard_map/factor/pallas_call | solution.py:419
Async XLA Ops:
  1.6 1.2 %copy-start = (bf16[4096,128]{1,0:T(8,128)(2,1)S(1)}, bf16[4096,128]{1,0:T(8,128)(2,1)}, u32[]{:S(2)}) copy-start(bf16[4096,128]{1,0:T(8,128)(2,1)} %omega_ref.1) | copy-start | bytes 3145732
  2.9 0.7 %copy-start.1 = (s32[1,4096]{1,0:T(1,128)S(1)}, s32[1,4096]{1,0:T(1,128)}, u32[]{:S(2)}) copy-start(s32[1,4096]{1,0:T(1,128)} %deg_ref.1) | copy-start | bytes 49156

commit v3 on v2

--- a/solution.py
+++ b/solution.py
@@ -14,7 +14,8 @@
 PAIR = 2 * TILE
 SPAN = PAIR + 2 * HALO
 FIELDS = SPAN // TILE
-BLOCK = 32
+BLOCK = 64
+PANEL = 16
 MESH = pl.DeviceIdType.MESH
 HIGHEST = lax.Precision.HIGHEST
 
@@ -334,9 +335,18 @@
         lo, hi = k * BLOCK, (k + 1) * BLOCK
         block = work[lo:hi, lo:hi]
         left = jnp.where(rows == cols, jnp.float32(1), jnp.float32(0))
-        for j in range(BLOCK - 1):
-            ratio = jnp.where(rows[:, :1] > j, block[:, j : j + 1] / block[j : j + 1, j : j + 1], 0.0)
-            block, left = (block - ratio * block[j : j + 1, :], left - ratio * left[j : j + 1, :])
+        for first in range(0, BLOCK, PANEL):
+            spread = [
+                jnp.broadcast_to(block[:, first + i : first + i + 1], (BLOCK, BLOCK)) for i in range(PANEL)
+            ]
+            for i in range(PANEL):
+                j = first + i
+                if j == BLOCK - 1:
+                    break
+                ratio = jnp.where(rows > j, spread[i] * (1.0 / spread[i][j : j + 1, :]), 0.0)
+                for later in range(i + 1, PANEL):
+                    spread[later] = spread[later] - ratio * spread[later][j : j + 1, :]
+                block, left = (block - ratio * block[j : j + 1, :], left - ratio * left[j : j + 1, :])
         pivots = jnp.sum(jnp.where(rows == cols, block, 0.0), axis=1, keepdims=True)
         left = left / jnp.sqrt(pivots)
         panel = jnp.dot(left, work[lo:hi, :], precision=HIGHEST, preferred_element_type=jnp.float32)

time: 69 us -> 51.6 us (0.75)
  Pallas kernels: 65.2 us -> 47.8 us
    pallas_call x1, Pallas kernels: 30 us -> 12.6 us  [shards(): pl.pallas_call(functools.partial(factor_kernel, math.sqrt(length * zs)),...]
where the time goes in v3:
time: 51.6 us; the launch traced here: 51.4 us
  Pallas kernels  47.8 us (93%)
  local copies, waits for them, and re-layouts  2.95 us (6%)
  between operations  0.65 us (1%)
    pallas_call x1, Pallas kernels, shards(): pl.pallas_call(functools.partial(sketch_kernel, zs, vs), out_shape=(jax.S...  35.2 us
    pallas_call x1, Pallas kernels, shards(): pl.pallas_call(functools.partial(factor_kernel, math.sqrt(length * zs)),...  12.6 us
    unnamed x5, local copies, waits for them, and re-layouts  2.95 us

profile of v3, /device:TPU:0, one launch (start us, length us, event | category | flops | bytes accessed | tf_op | source)
XLA Modules:
  0.0 51.4 jit_solution(10489534431833824618)
XLA Ops:
  0.6 1.0 %copy.5.ids_ref = s32[1,10,4096]{2,1,0:T(8,128)S(1)} copy(s32[1,10,4096]{2,0,1:T(1,128)} %param.4) | data formatting | bytes 327680 | tf_op args[1]
  1.6 0.0 copy-start
  1.7 1.2 %copy-done = bf16[4096,128]{1,0:T(8,128)(2,1)S(1)} copy-done((bf16[4096,128]{1,0:T(8,128)(2,1)S(1)}, bf16[4096,128]{1,0:T(8,128)(2,1)}, u32[]{:S(2)}) %copy-start) | copy-done | bytes 1048600
  2.9 0.0 copy-start.1
  2.9 0.7 %copy-done.1 = s32[1,4096]{1,0:T(1,128)S(1)} copy-done((s32[1,4096]{1,0:T(1,128)S(1)}, s32[1,4096]{1,0:T(1,128)}, u32[]{:S(2)}) %copy-start.1) | copy-done | bytes 16408
  3.6 35.2 %sketch.1 = (f32[256,2048]{1,0:T(8,128)S(1)}, f32[384,128]{1,0:T(8,128)S(1)}) custom-call(bf16[4096,128]{1,0:T(8,128)(2,1)S(1)} %copy-done, s32[1,10,4096]{2,1,0:T(8,128)S(1)} %copy.5.ids_ref, s32[1,4096]{1,0:T(1,128)S(1)} %copy-done.1), custom_call_target="tpu_custom_call" | custom-call | tf_op jit(solution)/shard_map/sketch/pallas_call | solution.py:390
  38.8 12.6 %factor.1 = (f32[2048,128]{1,0:T(8,128)}, f32[256,128]{1,0:T(8,128)}) custom-call(f32[384,128]{1,0:T(8,128)S(1)} %get-tuple-element.4.gram_ref, f32[256,2048]{1,0:T(8,128)S(1)} %get-tuple-element.5.both_ref), custom_call_target="tpu_custom_call" | custom-call | tf_op jit(solution)/shard_map/factor/pallas_call | solution.py:429
Async XLA Ops:
  1.6 1.2 %copy-start = (bf16[4096,128]{1,0:T(8,128)(2,1)S(1)}, bf16[4096,128]{1,0:T(8,128)(2,1)}, u32[]{:S(2)}) copy-start(bf16[4096,128]{1,0:T(8,128)(2,1)} %omega_ref.1) | copy-start | bytes 3145732
  2.9 0.7 %copy-start.1 = (s32[1,4096]{1,0:T(1,128)S(1)}, s32[1,4096]{1,0:T(1,128)}, u32[]{:S(2)}) copy-start(s32[1,4096]{1,0:T(1,128)} %deg_ref.1) | copy-start | bytes 49156

commit v4 on v3

--- a/solution.py
+++ b/solution.py
@@ -373,7 +373,7 @@
         basis_ref[pl.ds(spot, PAIR), :] = part.T
         return carry
 
-    lax.fori_loop(0, both_ref.shape[1] // PAIR, one, 0)
+    lax.fori_loop(0, both_ref.shape[1] // PAIR, one, 0, unroll=True)
 
 
 def shards(omega, neighbor_ids, degrees):

time: 51.6 us -> 49.9 us (0.967)
  Pallas kernels: 47.8 us -> 46 us
    pallas_call x1, Pallas kernels: 12.6 us -> 10.8 us  [shards(): pl.pallas_call(functools.partial(factor_kernel, math.sqrt(length * zs)),...]
where the time goes in v4:
time: 49.9 us; the launch traced here: 49.6 us
  Pallas kernels  46 us (92%)
  local copies, waits for them, and re-layouts  2.95 us (6%)
  between operations  0.65 us (1%)
    pallas_call x1, Pallas kernels, shards(): pl.pallas_call(functools.partial(sketch_kernel, zs, vs), out_shape=(jax.S...  35.2 us
    pallas_call x1, Pallas kernels, shards(): pl.pallas_call(functools.partial(factor_kernel, math.sqrt(length * zs)),...  10.8 us
    unnamed x5, local copies, waits for them, and re-layouts  2.95 us

profile of v4, /device:TPU:0, one launch (start us, length us, event | category | flops | bytes accessed | tf_op | source)
XLA Modules:
  0.0 49.6 jit_solution(3810464006022660414)
XLA Ops:
  0.6 1.0 %copy.5.ids_ref = s32[1,10,4096]{2,1,0:T(8,128)S(1)} copy(s32[1,10,4096]{2,0,1:T(1,128)} %param.4) | data formatting | bytes 327680 | tf_op args[1]
  1.6 0.0 copy-start
  1.7 1.2 %copy-done = bf16[4096,128]{1,0:T(8,128)(2,1)S(1)} copy-done((bf16[4096,128]{1,0:T(8,128)(2,1)S(1)}, bf16[4096,128]{1,0:T(8,128)(2,1)}, u32[]{:S(2)}) %copy-start) | copy-done | bytes 1048600
  2.9 0.0 copy-start.1
  2.9 0.7 %copy-done.1 = s32[1,4096]{1,0:T(1,128)S(1)} copy-done((s32[1,4096]{1,0:T(1,128)S(1)}, s32[1,4096]{1,0:T(1,128)}, u32[]{:S(2)}) %copy-start.1) | copy-done | bytes 16408
  3.6 35.2 %sketch.1 = (f32[256,2048]{1,0:T(8,128)S(1)}, f32[384,128]{1,0:T(8,128)S(1)}) custom-call(bf16[4096,128]{1,0:T(8,128)(2,1)S(1)} %copy-done, s32[1,10,4096]{2,1,0:T(8,128)S(1)} %copy.5.ids_ref, s32[1,4096]{1,0:T(1,128)S(1)} %copy-done.1), custom_call_target="tpu_custom_call" | custom-call | tf_op jit(solution)/shard_map/sketch/pallas_call | solution.py:390
  38.8 10.8 %factor.1 = (f32[2048,128]{1,0:T(8,128)}, f32[256,128]{1,0:T(8,128)}) custom-call(f32[384,128]{1,0:T(8,128)S(1)} %get-tuple-element.4.gram_ref, f32[256,2048]{1,0:T(8,128)S(1)} %get-tuple-element.5.both_ref), custom_call_target="tpu_custom_call" | custom-call | tf_op jit(solution)/shard_map/factor/pallas_call | solution.py:429
Async XLA Ops:
  1.6 1.2 %copy-start = (bf16[4096,128]{1,0:T(8,128)(2,1)S(1)}, bf16[4096,128]{1,0:T(8,128)(2,1)}, u32[]{:S(2)}) copy-start(bf16[4096,128]{1,0:T(8,128)(2,1)} %omega_ref.1) | copy-start | bytes 3145732
  2.9 0.7 %copy-start.1 = (s32[1,4096]{1,0:T(1,128)S(1)}, s32[1,4096]{1,0:T(1,128)}, u32[]{:S(2)}) copy-start(s32[1,4096]{1,0:T(1,128)} %deg_ref.1) | copy-start | bytes 49156
